TPU v7x, 256 devices: a whole 4x4x8 slice. The times are simulated.
256 devices in a mesh: space: 32 (over y, z_hi, core), vel: 8 (over x, z_lo).
Axes of the slice: x: 4, y: 4, z: 8 (z_hi: 4, z_lo: 2; z = z_hi * 2 + z_lo), core: 2. Of those that a mesh axis runs over, the one named last changes fastest.
Arguments:
- dist: float32 [13824, 16384], P('vel', 'space'), may hold values from 0.02 to 45, as said below
- free_stream: float32 [13824], P('vel'), may hold values from 0.36 to 14, as said below
- area_normal: float32 [18, 16384], P(None, 'space'), may hold values from -2.7 to 2.7
- cell_volume: float32 [16384], P('space'), may hold values from 0.5 to 2
- face_nbr: int32 [6, 16384], P(None, 'space'), may hold values from 0 to 1023
- face_type: int32 [6, 16384], P(None, 'space'), may hold values from 0 to 2, as said below
- send_list: int32 [4, 4096], P(None, 'space'), may hold values from 0 to 511
Outputs:
- dist_new: float32 [13824, 16384], P('vel', 'space')
Inputs may be any that keep to these rules, and one draw needn't show every extreme that they name: `dist`: every entry is positive. `free_stream`: every entry is positive. `face_nbr`: an entry s at or above 512 names received slot s - 512; entries are read only where face_type is 0. `face_type`: 0 interior or partition face, 1 inflow, 2 outflow. `send_list`: local cell numbers of the sending partition.
All inputs are finite; a program needn't handle non-finite values.
Results may differ from a plain program's by a relative error of at most 0.0003.
Values sent between devices are 32-bit elements; how exact they have to be, the bound alone decides.
A program may use at most 128 MiB of HBM per device.

v0:
```python
import math

import jax
import jax.numpy as jnp
from jax import lax
from jax.sharding import PartitionSpec as P

NODES = 24


CFL = 0.9
MU_REF = 60.0
OMEGA = 0.81
PRANDTL = 2.0 / 3.0
neighbour_steps = (1, -1, 2, -2)


def passed_along(block, axis, distance):
    devices = range(lax.axis_size(axis))
    route = [((i - distance) % len(devices), i) for i in devices]
    return lax.ppermute(block, axis, route)


def grid_speeds(vel_index):
    spacing = 24.0 / NODES
    half = (NODES - 1) / 2.0
    first = (vel_index // (NODES * NODES)).astype(jnp.float32)
    second = (vel_index // NODES % NODES).astype(jnp.float32)
    last_axis = (vel_index % NODES).astype(jnp.float32)
    return ((first - half) * spacing, (second - half) * spacing, (last_axis - half) * spacing)


def project(table, field):
    return jnp.dot(
        table, field, precision=lax.Precision.HIGHEST, preferred_element_type=jnp.float32
    )


def hydrodynamic_variables(integral_averages):
    specific_matter_amount = integral_averages[0]
    mean_gas_speed = [integral_averages[1 + axis] / specific_matter_amount for axis in range(3)]
    particle_contribution = mean_gas_speed[0] ** 2 + mean_gas_speed[1] ** 2 + mean_gas_speed[2] ** 2
    local_thermal_level = (
        2.0 * integral_averages[4] / specific_matter_amount - particle_contribution
    ) / 3.0
    return (specific_matter_amount, mean_gas_speed, local_thermal_level)


def local(dist, free_stream, area_normal, cell_volume, face_nbr, face_type, send_list):
    vel_local = dist.shape[0]
    cell_count = dist.shape[1]
    vel_index = lax.axis_index("vel") * vel_local + jnp.arange(vel_local, dtype=jnp.int32)
    speeds = grid_speeds(vel_index)
    spacing = 24.0 / NODES
    weight = spacing**3
    top_speed = (NODES - 1) / 2.0 * spacing * math.sqrt(3.0)
    normals = area_normal.reshape(6, 3, cell_count)
    face_areas = jnp.sqrt(jnp.sum(normals * normals, axis=1))
    cell_limit = cell_volume / (top_speed * jnp.sum(face_areas, axis=0))
    time_step = CFL * lax.pmin(jnp.min(cell_limit), "space")
    step_ratio = time_step / cell_volume
    outgoing = [jnp.take(dist, send_list[direction], axis=1) for direction in range(4)]
    arrived = [
        passed_along(outgoing[direction], "space", neighbour_steps[direction])
        for direction in range(4)
    ]
    columns = [speeds[axis][:, None] for axis in range(3)]
    speed_sq = speeds[0] ** 2 + speeds[1] ** 2 + speeds[2] ** 2
    base_table = (
        jnp.stack([jnp.ones_like(speeds[0]), speeds[0], speeds[1], speeds[2], 0.5 * speed_sq])
        * weight
    )
    invariant_quantities = lax.psum(project(base_table, dist), "vel")
    specific_matter_amount, mean_gas_speed, local_thermal_level = hydrodynamic_variables(
        invariant_quantities
    )
    rel_old = [columns[axis] - mean_gas_speed[axis] for axis in range(3)]
    rel_old_sq = rel_old[0] ** 2 + rel_old[1] ** 2 + rel_old[2] ** 2
    local_heat = jnp.stack(
        [0.5 * weight * jnp.sum(rel_old[axis] * rel_old_sq * dist, axis=0) for axis in range(3)]
    )
    heat_flux = lax.psum(local_heat, "vel")
    extended = jnp.concatenate([dist] + arrived, axis=1)
    flux_total = jnp.zeros_like(dist)
    for face_slot in range(6):
        normal_speed = (
            columns[0] * normals[face_slot, 0]
            + columns[1] * normals[face_slot, 1]
            + columns[2] * normals[face_slot, 2]
        )
        outside = jnp.take(extended, face_nbr[face_slot], axis=1)
        face_kind = face_type[face_slot]
        outside = jnp.where(
            face_kind == 0, outside, jnp.where(face_kind == 1, free_stream[:, None], dist)
        )
        flux_total = flux_total + jnp.where(
            normal_speed > 0, normal_speed * dist, normal_speed * outside
        )
    flux_moments = lax.psum(project(base_table, flux_total), "vel")
    new_moments = invariant_quantities - step_ratio[None, :] * flux_moments
    density_new, mean_new, temp_new = hydrodynamic_variables(new_moments)
    relax_time = MU_REF * temp_new**OMEGA / (density_new * temp_new)
    relax_ratio = time_step / relax_time
    rel_new = [columns[axis] - mean_new[axis] for axis in range(3)]
    rel_sq = rel_new[0] ** 2 + rel_new[1] ** 2 + rel_new[2] ** 2
    maxwell = (
        density_new * (2.0 * math.pi * temp_new) ** (-1.5) * jnp.exp(-rel_sq / (2.0 * temp_new))
    )
    along_heat = rel_new[0] * heat_flux[0] + rel_new[1] * heat_flux[1] + rel_new[2] * heat_flux[2]
    shakhov = maxwell * (
        1.0
        + (1.0 - PRANDTL)
        * along_heat
        / (5.0 * density_new * temp_new * temp_new)
        * (rel_sq / temp_new - 5.0)
    )
    transported = dist - step_ratio[None, :] * flux_total
    return (transported + relax_ratio * shakhov) / (1.0 + relax_ratio)


def solution(mesh):
    return jax.shard_map(
        local,
        mesh=mesh,
        in_specs=(
            P("vel", "space"),
            P("vel"),
            P(None, "space"),
            P("space"),
            P(None, "space"),
            P(None, "space"),
            P(None, "space"),
        ),
        out_specs=P("vel", "space"),
        check_vma=False,
    )
```

profile of v0, /device:TPU:1, one launch (start us, length us, event | category | flops | bytes accessed | tf_op | source)
XLA Modules:
  0.0 348.8 jit_solution(8675281157710099629)
XLA Ops:
  0.0 1.3 compare_and_fusion.6
  1.3 5.0 %copy.98 = f32[1728,512]{0,1:T(8,128)} copy(f32[1728,512]{1,0:T(8,128)} %param.11) | data formatting | bytes 7077888 | tf_op args[0]
  6.4 3.4 gather_fusion
  11.1 4.4 %collective-permute-start = (f32[1728,128]{1,0:T(8,128)}, f32[1728,128]{1,0:T(8,128)}, u32[]{:S(2)}, u32[]{:S(2)}) collective-permute-start(f32[1728,128]{1,0:T(8,128)} %copy.91), channel_id=1, source_target_pairs={{248,0},{0,8},{8,16},{16,24},{24,32},{32,40},{40,48},{48,56},{56,6... | collective-permute-start | bytes 2654216 | tf_op jit(solution)/shard_map/ppermute | solution.py:21
  15.5 3.4 gather_fusion.1
  19.0 1.2 copy.93
  20.3 3.4 gather_fusion.2
  25.0 4.2 %collective-permute-start.2 = (f32[1728,128]{1,0:T(8,128)}, f32[1728,128]{1,0:T(8,128)}, u32[]{:S(2)}, u32[]{:S(2)}) collective-permute-start(f32[1728,128]{1,0:T(8,128)} %copy.95), channel_id=1, source_target_pairs={{240,0},{248,8},{0,16},{8,24},{16,32},{24,40},{32,48},{40,56},{48,... | collective-permute-start | bytes 2654216 | tf_op jit(solution)/shard_map/ppermute | solution.py:21
  29.2 4.3 %gather_fusion.3 = f32[128,1728]{1,0:T(8,128)} fusion(f32[1728,512]{0,1:T(8,128)} %copy.98, s32[1024]{0:T(1024)S(1)} %pad_clamp_fusion.6), kind=kCustom, calls=%fused_computation.4.clone | custom fusion | bytes 1769984 | tf_op jit(solution)/shard_map/jit(_take)/gather | solution.py:62
  33.5 2.4 select_bitcast_fusion
  35.9 2.4 copy.97
  38.3 1.5 collective-permute-start.3
  47.0 1.4 reshape.240
  49.0 1.4 stack.4
  50.5 3.2 fusion.74
  53.7 48.3 %psum.21 = f32[5,512]{1,0:T(8,128)} all-reduce(f32[5,512]{1,0:T(8,128)} %fusion.74), channel_id=1, replica_groups=mesh['space'=32,'vel'=8] {'vel'}, use_global_device_ids=true, to_apply=%region_4.7 | all-reduce | flops 2560 | bytes 20480 | tf_op jit(solution)/shard_map/psum | solution.py:73
  102.9 3.0 fusion.21
  108.4 78.3 %pmin.7 = f32[]{:T(128)} all-reduce(f32[]{:T(128)} %fusion.69), channel_id=1, replica_groups=mesh['space'=32,'vel'=8] {'space'}, use_global_device_ids=true, to_apply=%region_3.4 | all-reduce | flops 1 | bytes 8 | tf_op jit(solution)/shard_map/pmin | solution.py:60
  187.4 1.3 broadcast_divide_fusion
  188.6 1.3 pad_clamp_fusion.4
  189.9 1.3 pad_clamp_fusion.2
  191.2 1.3 pad_clamp_fusion
  192.5 1.5 fusion.71
  194.1 4.1 %constant_dynamic-update-slice_fusion.4 = f32[1728,1024]{0,1:T(8,128)} fusion(f32[1728,512]{0,1:T(8,128)} %copy.98), kind=kLoop, calls=%fused_computation.102 | loop fusion | bytes 7208960
  199.5 2.4 copy.99
  201.9 2.4 copy.100
  204.3 2.5 copy.101
  206.8 2.2 constant_dynamic-update-slice_fusion.3
  209.0 2.2 constant_dynamic-update-slice_fusion.2
  212.2 2.4 copy.102
  214.6 2.2 constant_dynamic-update-slice_fusion
  216.8 8.1 %gather_fusion.4 = f32[512,1728]{1,0:T(8,128)} fusion(f32[1728,1024]{0,1:T(8,128)} %constant_dynamic-update-slice_fusion, s32[1024]{0:T(1024)} %get-tuple-element.89), kind=kCustom, calls=%fused_computation.1.clone | custom fusion | bytes 7079936 | tf_op jit(solution)/shard_map/jit(_take)/gather | solution.py:91
  224.9 5.1 %copy.103 = f32[512,1728]{0,1:T(8,128)} copy(f32[512,1728]{1,0:T(8,128)} %gather_fusion.4) | data formatting | bytes 7077888 | tf_op jit(solution)/shard_map/jit(_take)/gather | solution.py:91
  230.0 8.1 %gather_fusion.5 = f32[512,1728]{1,0:T(8,128)} fusion(f32[1728,1024]{0,1:T(8,128)} %constant_dynamic-update-slice_fusion, s32[1024]{0:T(1024)} %get-tuple-element.88), kind=kCustom, calls=%fused_computation.5.clone | custom fusion | bytes 7079936 | tf_op jit(solution)/shard_map/jit(_take)/gather | solution.py:91
  238.2 5.1 %copy.104 = f32[512,1728]{0,1:T(8,128)} copy(f32[512,1728]{1,0:T(8,128)} %gather_fusion.5) | data formatting | bytes 7077888 | tf_op jit(solution)/shard_map/jit(_take)/gather | solution.py:91
  243.3 8.1 %gather_fusion.6 = f32[512,1728]{1,0:T(8,128)} fusion(f32[1728,1024]{0,1:T(8,128)} %constant_dynamic-update-slice_fusion, s32[1024]{0:T(1024)} %get-tuple-element.87), kind=kCustom, calls=%fused_computation.6.clone | custom fusion | bytes 7079936 | tf_op jit(solution)/shard_map/jit(_take)/gather | solution.py:91
  251.4 5.1 %copy.105 = f32[512,1728]{0,1:T(8,128)} copy(f32[512,1728]{1,0:T(8,128)} %gather_fusion.6) | data formatting | bytes 7077888 | tf_op jit(solution)/shard_map/jit(_take)/gather | solution.py:91
  256.5 8.1 %gather_fusion.7 = f32[512,1728]{1,0:T(8,128)} fusion(f32[1728,1024]{0,1:T(8,128)} %constant_dynamic-update-slice_fusion, s32[1024]{0:T(1024)} %get-tuple-element.86), kind=kCustom, calls=%fused_computation.7.clone | custom fusion | bytes 7079936 | tf_op jit(solution)/shard_map/jit(_take)/gather | solution.py:91
  264.6 5.1 %copy.106 = f32[512,1728]{0,1:T(8,128)} copy(f32[512,1728]{1,0:T(8,128)} %gather_fusion.7) | data formatting | bytes 7077888 | tf_op jit(solution)/shard_map/jit(_take)/gather | solution.py:91
  269.7 8.1 %gather_fusion.8 = f32[512,1728]{1,0:T(8,128)} fusion(f32[1728,1024]{0,1:T(8,128)} %constant_dynamic-update-slice_fusion, s32[1024]{0:T(1024)} %get-tuple-element.85), kind=kCustom, calls=%fused_computation.8.clone | custom fusion | bytes 7079936 | tf_op jit(solution)/shard_map/jit(_take)/gather | solution.py:91
  277.9 5.1 %copy.107 = f32[512,1728]{0,1:T(8,128)} copy(f32[512,1728]{1,0:T(8,128)} %gather_fusion.8) | data formatting | bytes 7077888 | tf_op jit(solution)/shard_map/jit(_take)/gather | solution.py:91
  282.9 8.1 %gather_fusion.9 = f32[512,1728]{1,0:T(8,128)} fusion(f32[1728,1024]{0,1:T(8,128)} %constant_dynamic-update-slice_fusion, s32[1024]{0:T(1024)} %get-tuple-element.84), kind=kCustom, calls=%fused_computation.9.clone | custom fusion | bytes 7079936 | tf_op jit(solution)/shard_map/jit(_take)/gather | solution.py:91
  291.1 5.1 %copy.108 = f32[512,1728]{0,1:T(8,128)} copy(f32[512,1728]{1,0:T(8,128)} %gather_fusion.9) | data formatting | bytes 7077888 | tf_op jit(solution)/shard_map/jit(_take)/gather | solution.py:91
  296.1 14.8 %fusion.27 = f32[1728,512]{1,0:T(8,128)S(1)} fusion(f32[512,1728]{0,1:T(8,128)} %copy.108, f32[512,1728]{0,1:T(8,128)} %copy.107, f32[512,1728]{0,1:T(8,128)} %copy.106, f32[512,1728]{0,1:T(8,128)} %copy.105, f32[512,1728]{0,1:T(8,128)} %copy.104, f32[512,1728]{0,1:T(8,128)} %copy.103, f32[1728,512]{1,0:T(8,128)S(1)} %copy-done, f32[512]{0:T(512)} %bitcast.135, ...), kind=kLoop, calls=%fused_computation.50 | loop fusion | flops 68124672 | bytes 28385280 | tf_op jit(solution)/shard_map/add | solution.py:96
  310.9 1.8 copy-done.1
  312.7 2.4 fusion.75
  315.1 25.4 %all-reduce = (f32[5,512]{1,0:T(8,128)}, f32[3,512]{1,0:T(4,128)}) all-reduce(f32[5,512]{1,0:T(8,128)} %fusion.75, f32[3,512]{1,0:T(4,128)} %pad_maximum_fusion), channel_id=1, replica_groups=mesh['space'=32,'vel'=8] {'vel'}, use_global_device_ids=true, to_apply=%region_5.8 | all-reduce | flops 4096 | bytes 32768 | tf_op jit(solution)/shard_map/psum | solution.py:99
  342.1 6.7 %fusion.17 = f32[1728,512]{1,0:T(8,128)} fusion(f32[1728,512]{1,0:T(8,128)S(1)} %copy-done, f32[1728,512]{1,0:T(8,128)} %copy-done.1, f32[512]{0:T(512)S(1)} %bitcast.162, f32[512]{0:T(512)S(1)} %bitcast.166, f32[512]{0:T(512)S(1)} %bitcast.164, f32[512]{0:T(512)S(1)} %bitcast.160, f32[512]{0:T(512)S(1)} %bitcast.161, f32[512]{0:T(512)S(1)} %bitcast.159, ...), kind=kLoop, calls=%fused_computation.39 | loop fusion | flops 24772608 | bytes 10664192 | tf_op jit(solution)/shard_map/div | solution.py:118
  (64 shorter events, 18.1 us)
Async XLA Ops:
  11.1 188.4 %collective-permute-start = (f32[1728,128]{1,0:T(8,128)}, f32[1728,128]{1,0:T(8,128)}, u32[]{:S(2)}, u32[]{:S(2)}) collective-permute-start(f32[1728,128]{1,0:T(8,128)} %copy.91), channel_id=1, source_target_pairs={{248,0},{0,8},{8,16},{16,24},{24,32},{32,40},{40,48},{48,56},{56,6... | collective-permute-start | bytes 2654216 | tf_op jit(solution)/shard_map/ppermute | solution.py:21
  20.3 181.6 %collective-permute-start.1 = (f32[1728,128]{1,0:T(8,128)}, f32[1728,128]{1,0:T(8,128)}, u32[]{:S(2)}, u32[]{:S(2)}) collective-permute-start(f32[1728,128]{1,0:T(8,128)} %copy.93), channel_id=1, source_target_pairs={{8,0},{16,8},{24,16},{32,24},{40,32},{48,40},{56,48},{64,56},{72,6... | collective-permute-start | bytes 2654216 | tf_op jit(solution)/shard_map/ppermute | solution.py:21
  25.0 179.3 %collective-permute-start.2 = (f32[1728,128]{1,0:T(8,128)}, f32[1728,128]{1,0:T(8,128)}, u32[]{:S(2)}, u32[]{:S(2)}) collective-permute-start(f32[1728,128]{1,0:T(8,128)} %copy.95), channel_id=1, source_target_pairs={{240,0},{248,8},{0,16},{8,24},{16,32},{24,40},{32,48},{40,56},{48,... | collective-permute-start | bytes 2654216 | tf_op jit(solution)/shard_map/ppermute | solution.py:21
  33.5 6.3 %copy-start.5 = (s32[6,512]{1,0:T(8,128)S(1)}, s32[6,512]{1,0:T(8,128)}, u32[]{:S(2)}) copy-start(s32[6,512]{1,0:T(8,128)} %param.15) | copy-start | bytes 36868
  33.5 17.0 %copy-start = (f32[1728,512]{1,0:T(8,128)S(1)}, f32[1728,512]{1,0:T(8,128)}, u32[]{:S(2)}) copy-start(f32[1728,512]{1,0:T(8,128)} %param.11) | copy-start | bytes 10616836
  38.3 173.9 %collective-permute-start.3 = (f32[1728,128]{1,0:T(8,128)}, f32[1728,128]{1,0:T(8,128)}, u32[]{:S(2)}, u32[]{:S(2)}) collective-permute-start(f32[1728,128]{1,0:T(8,128)} %copy.97), channel_id=1, source_target_pairs={{16,0},{24,8},{32,16},{40,24},{48,32},{56,40},{64,48},{72,56},{80,... | collective-permute-start | bytes 2654216 | tf_op jit(solution)/shard_map/ppermute | solution.py:21
  101.9 5.2 %copy-start.4 = (f32[6,3,512]{2,1,0:T(4,128)S(1)}, f32[6,3,512]{2,1,0:T(4,128)}, u32[]{:S(2)}) copy-start(f32[6,3,512]{2,1,0:T(4,128)} %reshape.240) | copy-start | bytes 110596
  101.9 5.2 %copy-start.10 = (f32[512]{0:T(512)S(1)}, f32[512]{0:T(512)}, u32[]{:S(2)}) copy-start(f32[512]{0:T(512)} %param.14) | copy-start | bytes 6148
  194.1 4.1 %copy-start.7 = (f32[512]{0:T(512)S(1)}, f32[512]{0:T(512)}, u32[]{:S(2)}) copy-start(f32[512]{0:T(512)} %broadcast_multiply_fusion.2) | copy-start | bytes 6148
  194.1 4.1 %copy-start.8 = (f32[512]{0:T(512)S(1)}, f32[512]{0:T(512)}, u32[]{:S(2)}) copy-start(f32[512]{0:T(512)} %broadcast_multiply_fusion.1) | copy-start | bytes 6148
  194.1 4.1 %copy-start.9 = (f32[512]{0:T(512)S(1)}, f32[512]{0:T(512)}, u32[]{:S(2)}) copy-start(f32[512]{0:T(512)} %broadcast_multiply_fusion) | copy-start | bytes 6148
  194.1 4.7 %copy-start.6 = (s32[6,512]{1,0:T(8,128)S(1)}, s32[6,512]{1,0:T(8,128)}, u32[]{:S(2)}) copy-start(s32[6,512]{1,0:T(8,128)} %param.16) | copy-start | bytes 36868
  206.8 4.4 %copy-start.2 = (f32[1728,128]{0,1:T(8,128)S(1)}, f32[1728,128]{0,1:T(8,128)}, u32[]{:S(2)}) copy-start(f32[1728,128]{0,1:T(8,128)} %copy.101) | copy-start | bytes 2654212
  296.1 16.6 %copy-start.3 = (f32[5,1728]{1,0:T(8,128)S(1)}, f32[5,1728]{1,0:T(8,128)}, u32[]{:S(2)}) copy-start(f32[5,1728]{1,0:T(8,128)} %stack.4) | copy-start | bytes 103684
  310.9 1.8 copy-start.1
where the time goes:
time: 355 us; the launch traced here: 349 us
  blocking collectives  152 us (43%)
  local copies, waits for them, and re-layouts  134 us (38%)
  other arithmetic  46.5 us (13%)
  starting transfers between devices  10.1 us (3%)
  matrix products  5.56 us (2%)
    gather x12, local copies, waits for them, and re-layouts, local(): outside = jnp.take(extended, face_nbr[face_slot], axis=1)  79.3 us
    pmin x1, blocking collectives, local(): time_step = CFL * lax.pmin(jnp.min(cell_limit), 'space')  78.3 us
    psum x1, blocking collectives, local(): invariant_quantities = lax.psum(project(base_table, dist), 'vel')  48.3 us
    psum x1, blocking collectives, local(): flux_moments = lax.psum(project(base_table, flux_total), 'vel')  25.4 us
    unnamed x27, local copies, waits for them, and re-layouts  16.4 us
    add x1, other arithmetic, local(): flux_total + jnp.where(normal_speed > 0, normal_speed * dist, normal_spee...  14.8 us
    gather x4, local copies, waits for them, and re-layouts, local(): jnp.take(dist, send_list[direction], axis=1)  14.4 us
    ppermute x4, starting transfers between devices, passed_along(): return lax.ppermute(block, axis, route)  10.1 us
  transfers between devices with their start and end apart: 4, of which 0 were waited for; matrix products, arithmetic and copies ran while one was open for 18% of the time, Pallas kernels for 0%

commit v1 on v0

v1 whole, which is shorter than its diff:
```python
import functools
import math

import jax
import jax.numpy as jnp
from jax import lax
from jax.experimental import pallas as pl
from jax.experimental.pallas import tpu as pltpu
from jax.sharding import PartitionSpec as P

MESH = pl.DeviceIdType.MESH
F32 = jnp.float32
BF16 = jnp.bfloat16

NODES = 24
HALF = (NODES - 1) / 2.0
TOP_SPEED = HALF * math.sqrt(3.0)
CFL = 0.9
MU_REF = 60.0
OMEGA = 0.81
PRANDTL = 2.0 / 3.0
STEPS = (1, -1, 2, -2)

VELS = 1728
CELLS = 512
SEND = 128
CHUNK = 144
CHUNKS = VELS // CHUNK
GROUPS = CHUNK // NODES


def two_parts(x):
    high = x.astype(BF16)
    low = (x - high.astype(F32)).astype(BF16)
    return high, low


def fold(x):
    return x[0:8] + x[8:16] + x[16:24]


def group_speeds(vel, group):
    first = (vel * 3 + group // NODES).astype(F32) - HALF
    second = (group % NODES).astype(F32) - HALF
    return first, second


def one_hot(rows, base, wanted):
    ids = lax.broadcasted_iota(jnp.int32, (rows, wanted.shape[1]), 0) + base
    return jnp.where(ids == wanted, 1.0, 0.0).astype(BF16)


def transport(
    n_space,
    dist_hbm,
    stream_ref,
    area_ref,
    volume_ref,
    nbr_ref,
    type_ref,
    list_ref,
    moved,
    coef_ref,
    dist_v,
    parts,
    outgoing,
    arrived,
    picks,
    send_picks,
    gathered,
    arrived_parts,
    normal,
    slope,
    inflow,
    source,
    stream_b,
    sums,
    old_msg,
    old_in,
    old_msg2,
    old_in2,
    new_msg,
    new_in,
    min_msg,
    min_in,
    min_msg2,
    min_in2,
    load_sem,
    send_sem,
    recv_sem,
    small_send,
    small_recv,
):
    s = lax.axis_index("space")
    v = lax.axis_index("vel")
    near = 8
    far = n_space // near
    partners = [lax.rem(s + step + n_space, n_space) for step in STEPS]
    near_peers = [(s // near) * near + lax.rem(s + i, near) for i in range(1, near)]
    far_peers = [lax.rem(s + near * i, n_space) for i in range(1, far)]
    vel_peers = [lax.rem(v + i, 8) for i in range(1, 8)]
    x_peers = [lax.rem(v + 2 * i, 8) for i in range(1, 4)]
    z_peer = v + 1 - 2 * lax.rem(v, 2)

    barrier = pltpu.get_barrier_semaphore()
    greeted = [(q, v) for q in partners + near_peers + far_peers]
    greeted += [(s, q) for q in vel_peers]
    for q in greeted:
        pl.semaphore_signal(barrier, inc=1, device_id=q, device_id_type=MESH)

    def load(c):
        rows = pl.ds(pl.multiple_of(c * CHUNK, CHUNK), CHUNK)
        return pltpu.make_async_copy(dist_hbm.at[rows], dist_v.at[rows], load_sem.at[c])

    def send(c, d):
        rows = pl.ds(pl.multiple_of(c * CHUNK, CHUNK), CHUNK)
        return pltpu.make_async_remote_copy(
            src_ref=outgoing.at[d, rows],
            dst_ref=arrived.at[d, rows],
            send_sem=send_sem.at[c, d],
            recv_sem=recv_sem.at[c, d],
            device_id=(partners[d], v),
            device_id_type=MESH,
        )

    def small(src, dst, at, where):
        return pltpu.make_async_remote_copy(
            src_ref=src,
            dst_ref=dst,
            send_sem=small_send.at[at],
            recv_sem=small_recv.at[at],
            device_id=where,
            device_id_type=MESH,
        )

    near_copies = [
        small(min_msg, min_in.at[i], i, (near_peers[i], v)) for i in range(near - 1)
    ]
    far_copies = [
        small(min_msg2, min_in2.at[i], 7 + i, (far_peers[i], v)) for i in range(far - 1)
    ]
    x_copies = [small(old_msg, old_in.at[i], 10 + i, (s, x_peers[i])) for i in range(3)]
    z_copy = small(old_msg2, old_in2, 13, (s, z_peer))
    new_copies = [
        small(new_msg, new_in.at[i], 14 + i, (s, vel_peers[i])) for i in range(7)
    ]

    for c in range(CHUNKS):
        load(c).start()

    send_picks[...] = one_hot(
        CELLS, 0, jnp.concatenate([list_ref[d : d + 1, :] for d in range(4)], axis=1)
    )

    def pack(c):
        rows = pl.ds(pl.multiple_of(c * CHUNK, CHUNK), CHUNK)
        high, low = two_parts(dist_v[rows, :])
        parts[c, 0:CHUNK, :] = high
        parts[c, CHUNK : 2 * CHUNK, :] = low
        both = jnp.dot(parts[c], send_picks[...], preferred_element_type=F32)
        picked = both[0:CHUNK] + both[CHUNK : 2 * CHUNK]
        for d in range(4):
            outgoing[d, rows, :] = picked[:, d * SEND : (d + 1) * SEND]

    load(0).wait()
    pack(0)
    pl.semaphore_wait(barrier, len(greeted))
    for d in range(4):
        send(0, d).start()

    def pack_and_send(c, _):
        load(c).wait()
        pack(c)
        for d in range(4):
            send(c, d).start()
        return 0

    lax.fori_loop(1, CHUNKS, pack_and_send, 0)

    normal[...] = jnp.zeros_like(normal)
    for k in range(6):
        for axis in range(3):
            normal[axis, k : k + 1, :] = area_ref[3 * k + axis : 3 * k + axis + 1, :]
    areas = jnp.sqrt(normal[0] * normal[0] + normal[1] * normal[1] + normal[2] * normal[2])
    volume = volume_ref[...]
    limit = volume / (TOP_SPEED * jnp.sum(areas, axis=0, keepdims=True))
    least = jnp.minimum(
        jnp.minimum(limit[:, 0:128], limit[:, 128:256]),
        jnp.minimum(limit[:, 256:384], limit[:, 384:512]),
    )
    min_msg[...] = jnp.broadcast_to(least, (8, 128))
    for copy in near_copies:
        copy.start()

    speed = lax.broadcasted_iota(jnp.int32, (NODES, CELLS), 0).astype(F32) - HALF
    for k in range(6):
        slope[k] = speed * normal[2, k : k + 1, :]
    for axis in range(3):
        normal[axis, 6:7, :] = jnp.sum(normal[axis, 0:6, :], axis=0, keepdims=True)
    slope[6] = speed * normal[2, 6:7, :]
    kind = type_ref[...]
    cell_ids = lax.broadcasted_iota(jnp.int32, (6, CELLS), 1)
    source[0:6, :] = jnp.where(kind == 0, nbr_ref[...], jnp.where(kind == 2, cell_ids, -1))
    inflow[0:6, :] = jnp.where(kind == 1, 1.0, 0.0)

    for i in range(14):
        start = min(i * 128, VELS - 128)
        row = stream_ref[:, start : start + 128]
        stream_b[start : start + 128, :] = jnp.broadcast_to(row, (128, 128)).T

    def fill(i, _):
        k = i // 8
        base = (i % 8) * 128
        picks[k, pl.ds(pl.multiple_of(base, 128), 128), :] = one_hot(
            128, base, source[pl.ds(k, 1), :]
        )
        return 0

    lax.fori_loop(0, 48, fill, 0)

    sums[...] = jnp.zeros_like(sums)

    def old_moments(group, _):
        rows = pl.ds(pl.multiple_of(group * NODES, NODES), NODES)
        cx, cy = group_speeds(v, group)
        d = dist_v[rows, :]
        d1 = d * speed
        d2 = d1 * speed
        d3 = d2 * speed
        s0, s1, s2, s3 = fold(d), fold(d1), fold(d2), fold(d3)
        sq = cx * cx + cy * cy
        r0 = sq * s0 + s2
        terms = (
            s0,
            cx * s0,
            cy * s0,
            s1,
            (cx * cx) * s0,
            (cy * cy) * s0,
            s2,
            (cx * cy) * s0,
            cx * s1,
            cy * s1,
            cx * r0,
            cy * r0,
            sq * s1 + s3,
        )
        for i, term in enumerate(terms):
            sums[i] += term
        return 0

    lax.fori_loop(0, VELS // NODES, old_moments, 0)
    old_msg[...] = jnp.zeros_like(old_msg)
    for i in range(13):
        old_msg[i : i + 1, :] = jnp.sum(sums[i], axis=0, keepdims=True)
    for copy in x_copies:
        copy.start()
    for copy in near_copies:
        copy.wait()
    lowest = min_msg[...]
    for i in range(near - 1):
        lowest = jnp.minimum(lowest, min_in[i])
    min_msg2[...] = lowest
    for copy in far_copies:
        copy.start()

    def products(lhs, half):
        for k in range(6):
            gathered[k] = jnp.dot(
                lhs, picks[k, half * CELLS : (half + 1) * CELLS, :], preferred_element_type=F32
            )

    def picked_rows(k, g):
        one = pl.ds(pl.multiple_of(g * NODES, NODES), NODES)
        two = pl.ds(pl.multiple_of(CHUNK + g * NODES, NODES), NODES)
        return gathered[k, one, :] + gathered[k, two, :]

    def normal_speed(k, cx, cy):
        return (cx * normal[0, k : k + 1, :] + cy * normal[1, k : k + 1, :]) + slope[k]

    def local_flux(c, _):
        products(parts[c], 0)

        def one_group(g, _):
            group = c * GROUPS + g
            rows = pl.ds(pl.multiple_of(group * NODES, NODES), NODES)
            cx, cy = group_speeds(v, group)
            inward = jnp.zeros((NODES, CELLS), F32)
            free = jnp.zeros((NODES, CELLS), F32)
            total = jnp.zeros((NODES, CELLS), F32)
            for k in range(6):
                u = jnp.minimum(normal_speed(k, cx, cy), 0.0)
                inward += u
                free += u * inflow[k : k + 1, :]
                total += u * picked_rows(k, g)
            stream = stream_b[rows, :]
            stream = jnp.concatenate([stream] * 4, axis=1)
            outward = normal_speed(6, cx, cy) - inward
            moved[rows, :] = outward * dist_v[rows, :] + total + free * stream
            return 0

        lax.fori_loop(0, GROUPS, one_group, 0)
        return 0

    lax.fori_loop(0, CHUNKS, local_flux, 0)

    for copy in x_copies:
        copy.wait()
    old_msg2[...] = old_msg[...] + old_in[0] + old_in[1] + old_in[2]
    z_copy.start()
    for copy in far_copies:
        copy.wait()
    lowest = min_msg2[...]
    for i in range(far - 1):
        lowest = jnp.minimum(lowest, min_in2[i])
    time_step = CFL * jnp.min(lowest[0:1, :], axis=1, keepdims=True)
    time_step = jnp.broadcast_to(time_step, (1, CELLS))
    ratio = time_step / volume

    for i in range(5):
        sums[i] = jnp.zeros((8, CELLS), F32)

    def remote_flux(c, _):
        rows = pl.ds(pl.multiple_of(c * CHUNK, CHUNK), CHUNK)
        for d in range(4):
            send(c, d).wait_recv()
        for d in range(4):
            high, low = two_parts(arrived[d, rows, :])
            lanes = slice(d * SEND, (d + 1) * SEND)
            arrived_parts[0:CHUNK, lanes] = high
            arrived_parts[CHUNK : 2 * CHUNK, lanes] = low
        products(arrived_parts[...], 1)

        def one_group(g, _):
            group = c * GROUPS + g
            own = pl.ds(pl.multiple_of(group * NODES, NODES), NODES)
            cx, cy = group_speeds(v, group)
            total = moved[own, :]
            for k in range(6):
                u = jnp.minimum(normal_speed(k, cx, cy), 0.0)
                total += u * picked_rows(k, g)
            t = dist_v[own, :] - ratio * total
            moved[own, :] = t
            t1 = t * speed
            s0, s1, s2 = fold(t), fold(t1), fold(t1 * speed)
            sums[0] += s0
            sums[1] += cx * s0
            sums[2] += cy * s0
            sums[3] += s1
            sums[4] += 0.5 * ((cx * cx + cy * cy) * s0 + s2)
            return 0

        lax.fori_loop(0, GROUPS, one_group, 0)
        return 0

    lax.fori_loop(0, CHUNKS, remote_flux, 0)

    new_msg[...] = jnp.zeros_like(new_msg)
    for i in range(5):
        new_msg[i : i + 1, :] = jnp.sum(sums[i], axis=0, keepdims=True)
    for copy in new_copies:
        copy.start()

    z_copy.wait()
    old = old_msg2[...] + old_in2[...]
    rho = old[0:1]
    mean = [old[1 + i : 2 + i] / rho for i in range(3)]
    pressure = [[old[4:5], old[7:8], old[8:9]], [old[7:8], old[5:6], old[9:10]], [old[8:9], old[9:10], old[6:7]]]
    trace = old[4:5] + old[5:6] + old[6:7]
    mean_sq = mean[0] * mean[0] + mean[1] * mean[1] + mean[2] * mean[2]
    for i in range(3):
        along = (
            mean[0] * pressure[i][0] + mean[1] * pressure[i][1] + mean[2] * pressure[i][2]
        )
        coef_ref[8 + i : 9 + i, :] = 0.5 * (
            old[10 + i : 11 + i] - 2.0 * along - mean[i] * trace + 2.0 * rho * mean_sq * mean[i]
        )
    coef_ref[11:12, :] = time_step
    coef_ref[12:16, :] = jnp.zeros((4, CELLS), F32)

    def finish_sends(c, _):
        for d in range(4):
            send(c, d).wait_send()
        return 0

    lax.fori_loop(0, CHUNKS, finish_sends, 0)
    for copy in new_copies:
        copy.wait()
    total = new_msg[...]
    for i in range(7):
        total = total + new_in[i]
    coef_ref[0:8, :] = total


def relax(moved, coef_ref, out_hbm, result, first, second, third, sem):
    v = lax.axis_index("vel")
    rho = coef_ref[0:1, :]
    mean = [coef_ref[1 + i : 2 + i, :] / rho for i in range(3)]
    heat = [coef_ref[8 + i : 9 + i, :] for i in range(3)]
    time_step = coef_ref[11:12, :]
    mean_sq = mean[0] * mean[0] + mean[1] * mean[1] + mean[2] * mean[2]
    temp = (2.0 * coef_ref[4:5, :] / rho - mean_sq) / 3.0
    relax_time = MU_REF * jnp.exp(OMEGA * jnp.log(temp)) / (rho * temp)
    relax_ratio = time_step / relax_time
    keep = 1.0 / (1.0 + relax_ratio)
    cold = 1.0 / temp
    root = lax.rsqrt(2.0 * math.pi * temp)
    scale = relax_ratio * keep * rho * (root * root * root)
    bend = (1.0 - PRANDTL) / (5.0 * rho * temp * temp)
    speed = lax.broadcasted_iota(jnp.int32, (NODES, CELLS), 0).astype(F32) - HALF
    for axis, table in ((1, second), (2, third)):
        rel = speed - mean[axis]
        sq = rel * rel * cold
        table[0] = jnp.exp(-0.5 * sq)
        table[1] = sq
        table[2] = rel * (heat[axis] * bend)
    own = lax.broadcasted_iota(jnp.int32, (8, CELLS), 0).astype(F32) - HALF
    rel = own + (v * 3).astype(F32) - mean[0]
    sq = rel * rel * cold
    first[0] = jnp.exp(-0.5 * sq) * scale
    first[1] = sq - 5.0
    first[2] = rel * (heat[0] * bend)

    def one_chunk(c, _):
        def one_group(g, _):
            group = c * GROUPS + g
            rows = pl.ds(pl.multiple_of(group * NODES, NODES), NODES)
            a = pl.ds(group // NODES, 1)
            b = pl.ds(group % NODES, 1)
            weight = first[0, a, :] * second[0, b, :]
            sq = (first[1, a, :] + second[1, b, :]) + third[1]
            along = (first[2, a, :] + second[2, b, :]) + third[2]
            gauss = weight * third[0]
            result[rows, :] = moved[rows, :] * keep + gauss * (1.0 + along * sq)
            return 0

        lax.fori_loop(0, GROUPS, one_group, 0)
        rows = pl.ds(pl.multiple_of(c * CHUNK, CHUNK), CHUNK)
        pltpu.make_async_copy(result.at[rows], out_hbm.at[rows], sem.at[c]).start()
        return 0

    lax.fori_loop(0, CHUNKS, one_chunk, 0)

    def finish(c, _):
        rows = pl.ds(pl.multiple_of(c * CHUNK, CHUNK), CHUNK)
        pltpu.make_async_copy(result.at[rows], out_hbm.at[rows], sem.at[c]).wait()
        return 0

    lax.fori_loop(0, CHUNKS, finish, 0)


def solution(mesh):
    n_space = mesh.shape["space"]
    vmem = pl.BlockSpec(memory_space=pltpu.VMEM)
    hbm = pl.BlockSpec(memory_space=pl.ANY)

    def local(dist, free_stream, area_normal, cell_volume, face_nbr, face_type, send_list):
        moved, coef = pl.pallas_call(
            functools.partial(transport, n_space),
            out_shape=(
                jax.ShapeDtypeStruct((VELS, CELLS), F32),
                jax.ShapeDtypeStruct((16, CELLS), F32),
            ),
            in_specs=[hbm] + [vmem] * 6,
            out_specs=(vmem, vmem),
            scratch_shapes=[
                pltpu.VMEM((VELS, CELLS), F32),
                pltpu.VMEM((CHUNKS, 2 * CHUNK, CELLS), BF16),
                pltpu.VMEM((4, VELS, SEND), F32),
                pltpu.VMEM((4, VELS, SEND), F32),
                pltpu.VMEM((6, 2 * CELLS, CELLS), BF16),
                pltpu.VMEM((CELLS, CELLS), BF16),
                pltpu.VMEM((6, 2 * CHUNK, CELLS), F32),
                pltpu.VMEM((2 * CHUNK, CELLS), BF16),
                pltpu.VMEM((3, 8, CELLS), F32),
                pltpu.VMEM((7, NODES, CELLS), F32),
                pltpu.VMEM((8, CELLS), F32),
                pltpu.VMEM((8, CELLS), jnp.int32),
                pltpu.VMEM((VELS, 128), F32),
                pltpu.VMEM((13, 8, CELLS), F32),
                pltpu.VMEM((16, CELLS), F32),
                pltpu.VMEM((3, 16, CELLS), F32),
                pltpu.VMEM((16, CELLS), F32),
                pltpu.VMEM((16, CELLS), F32),
                pltpu.VMEM((8, CELLS), F32),
                pltpu.VMEM((7, 8, CELLS), F32),
                pltpu.VMEM((8, 128), F32),
                pltpu.VMEM((7, 8, 128), F32),
                pltpu.VMEM((8, 128), F32),
                pltpu.VMEM((max(1, n_space // 8 - 1), 8, 128), F32),
                pltpu.SemaphoreType.DMA((CHUNKS,)),
                pltpu.SemaphoreType.DMA((CHUNKS, 4)),
                pltpu.SemaphoreType.DMA((CHUNKS, 4)),
                pltpu.SemaphoreType.DMA((21,)),
                pltpu.SemaphoreType.DMA((21,)),
            ],
            compiler_params=pltpu.CompilerParams(
                collective_id=0, has_side_effects=True, vmem_limit_bytes=44 * 2**20
            ),
            name="transport",
        )(
            dist,
            free_stream.reshape(1, VELS),
            area_normal,
            cell_volume.reshape(1, CELLS),
            face_nbr,
            face_type,
            send_list,
        )
        return pl.pallas_call(
            relax,
            out_shape=jax.ShapeDtypeStruct((VELS, CELLS), F32),
            in_specs=[vmem, vmem],
            out_specs=hbm,
            scratch_shapes=[
                pltpu.VMEM((VELS, CELLS), F32),
                pltpu.VMEM((3, 8, CELLS), F32),
                pltpu.VMEM((3, NODES, CELLS), F32),
                pltpu.VMEM((3, NODES, CELLS), F32),
                pltpu.SemaphoreType.DMA((CHUNKS,)),
            ],
            compiler_params=pltpu.CompilerParams(vmem_limit_bytes=24 * 2**20),
            name="relax",
        )(moved, coef)

    return jax.shard_map(
        local,
        mesh=mesh,
        in_specs=(
            P("vel", "space"),
            P("vel"),
            P(None, "space"),
            P("space"),
            P(None, "space"),
            P(None, "space"),
            P(None, "space"),
        ),
        out_specs=P("vel", "space"),
        check_vma=False,
    )
```

time: 355 us -> 125 us (0.35); the launches traced: 349 us -> 125 us
  blocking collectives: 152 us -> 0 us
  local copies, waits for them, and re-layouts: 134 us -> 6.3 us
  Pallas kernels: 0 us -> 119 us
  other arithmetic: 46.5 us -> 0 us
  starting transfers between devices: 10.1 us -> 0 us
  matrix products: 5.56 us -> 0 us
    pallas_call x0 -> x2, Pallas kernels: none -> 119 us  [the longest x1 115 us: local(): pl.pallas_call(functools.partial(transport, n_space), out_shape=(jax.Shap...]
    gather x16 -> x0, local copies, waits for them, and re-layouts: 93.8 us -> none  [the longest x12 79.3 us: local(): outside = jnp.take(extended, face_nbr[face_slot], axis=1)]
    pmin x1 -> x0, blocking collectives: 78.3 us -> none  [local(): time_step = CFL * lax.pmin(jnp.min(cell_limit), 'space')]
    psum x2 -> x0, blocking collectives: 73.6 us -> none  [the longest x1 48.3 us: local(): invariant_quantities = lax.psum(project(base_table, dist), 'vel')]
    add x2 -> x0, other arithmetic: 14.8 us -> none  [the longest x1 14.8 us: local(): flux_total + jnp.where(normal_speed > 0, normal_speed * dist, normal_spee...]
    unnamed x27 -> x12, local copies, waits for them, and re-layouts: 16.4 us -> 5.59 us
    ppermute x4 -> x0, starting transfers between devices: 10.1 us -> none  [passed_along(): return lax.ppermute(block, axis, route)]
    ppermute x4 -> x0, local copies, waits for them, and re-layouts: 9.63 us -> none  [passed_along(): return lax.ppermute(block, axis, route)]
  transfers between devices with their start and end apart: 4 -> 0, of which waited for: 0 -> 0; matrix products, arithmetic and copies ran while one was open for 18% -> 0% of each run, Pallas kernels for 0% -> 0%
where the time goes in v1:
time: 125 us
  Pallas kernels  119 us (95%)
  local copies, waits for them, and re-layouts  6.3 us (5%)
    pallas_call x1, Pallas kernels, local(): pl.pallas_call(functools.partial(transport, n_space), out_shape=(jax.Shap...  115 us
    unnamed x12, local copies, waits for them, and re-layouts  5.59 us
    pallas_call x1, Pallas kernels, local(): pl.pallas_call(relax, out_shape=jax.ShapeDtypeStruct((VELS, CELLS), F32),...  3.32 us

profile of v1, /device:TPU:1, one launch (start us, length us, event | category | flops | bytes accessed | tf_op | source)
XLA Modules:
  0.0 124.9 jit_solution(16486240251186158794)
XLA Ops:
  0.0 0.7 reshape.6.stream_ref
  0.7 0.0 copy-start
  0.7 2.0 %copy-done = f32[1728,512]{1,0:T(8,128)S(1)} copy-done((f32[1728,512]{1,0:T(8,128)S(1)}, f32[1728,512]{1,0:T(8,128)}, u32[]{:S(2)}) %copy-start) | copy-done | bytes 3538968
  2.7 0.0 copy-start.1
  2.7 0.8 copy-done.1
  3.5 0.0 copy-start.2
  3.5 0.7 copy-done.2
  4.2 0.0 copy-start.3
  4.2 0.7 copy-done.3
  4.9 0.0 copy-start.4
  4.9 0.7 copy-done.4
  5.6 0.0 copy-start.5
  5.6 0.7 copy-done.5
  6.3 115.3 %transport.1 = (f32[1728,512]{1,0:T(8,128)S(1)}, f32[16,512]{1,0:T(8,128)S(1)}) custom-call(f32[1728,512]{1,0:T(8,128)S(1)} %copy-done, f32[1,1728]{1,0:T(1,128)S(1)} %reshape.6.stream_ref, f32[18,512]{1,0:T(8,128)S(1)} %copy-done.1, f32[1,512]{1,0:T(1,128)S(1)} %bitcast.1, s32[6,512]{1,0:T(8,128)S(1)} %copy-done.2, s32[6,512]{1,0:T(8,128)S(1)} %copy-done.3, ...), custom_call_target="tpu_custom_call" | custom-call | tf_op jit(solution)/shard_map/transport/pallas_call | solution.py:458
  121.6 3.3 %relax.1 = f32[1728,512]{1,0:T(8,128)} custom-call(f32[1728,512]{1,0:T(8,128)S(1)} %get-tuple-element.7.moved, f32[16,512]{1,0:T(8,128)S(1)} %get-tuple-element.8.coef_ref), custom_call_target="tpu_custom_call" | custom-call | tf_op jit(solution)/shard_map/relax/pallas_call | solution.py:510
Async XLA Ops:
  0.7 2.0 %copy-start = (f32[1728,512]{1,0:T(8,128)S(1)}, f32[1728,512]{1,0:T(8,128)}, u32[]{:S(2)}) copy-start(f32[1728,512]{1,0:T(8,128)} %dist_hbm.1) | copy-start | bytes 10616836
  2.7 0.8 copy-start.1
  3.5 0.7 copy-start.2
  4.2 0.7 copy-start.3
  4.9 0.7 copy-start.4
  5.6 0.7 copy-start.5

commit v2 on v1

--- a/solution.py
+++ b/solution.py
@@ -27,6 +27,8 @@
 CHUNK = 144
 CHUNKS = VELS // CHUNK
 GROUPS = CHUNK // NODES
+WINDOW = 3
+AHEAD = 2
 
 
 def two_parts(x):
@@ -53,14 +55,20 @@
 def transport(
     n_space,
     dist_hbm,
+    stream_hbm,
+    area_hbm,
+    volume_hbm,
+    nbr_hbm,
+    type_hbm,
+    list_hbm,
+    moved,
+    coef_ref,
     stream_ref,
     area_ref,
     volume_ref,
     nbr_ref,
     type_ref,
     list_ref,
-    moved,
-    coef_ref,
     dist_v,
     parts,
     outgoing,
@@ -86,6 +94,7 @@
     min_msg2,
     min_in2,
     load_sem,
+    input_sem,
     send_sem,
     recv_sem,
     small_send,
@@ -145,9 +154,27 @@
         small(new_msg, new_in.at[i], 14 + i, (s, vel_peers[i])) for i in range(7)
     ]
 
-    for c in range(CHUNKS):
+    inputs = [
+        pltpu.make_async_copy(src, dst, input_sem.at[i])
+        for i, (src, dst) in enumerate(
+            (
+                (list_hbm, list_ref),
+                (area_hbm, area_ref),
+                (volume_hbm, volume_ref),
+                (nbr_hbm, nbr_ref),
+                (type_hbm, type_ref),
+                (stream_hbm, stream_ref),
+            )
+        )
+    ]
+    inputs[0].start()
+    load(0).start()
+    for copy in inputs[1:]:
+        copy.start()
+    for c in range(1, CHUNKS):
         load(c).start()
 
+    inputs[0].wait()
     send_picks[...] = one_hot(
         CELLS, 0, jnp.concatenate([list_ref[d : d + 1, :] for d in range(4)], axis=1)
     )
@@ -162,35 +189,43 @@
         for d in range(4):
             outgoing[d, rows, :] = picked[:, d * SEND : (d + 1) * SEND]
 
+    def start_sends(c):
+        for d in range(4):
+            send(c, d).start()
+
     load(0).wait()
     pack(0)
-    pl.semaphore_wait(barrier, len(greeted))
-    for d in range(4):
-        send(0, d).start()
-
-    def pack_and_send(c, _):
-        load(c).wait()
-        pack(c)
-        for d in range(4):
-            send(c, d).start()
-        return 0
-
-    lax.fori_loop(1, CHUNKS, pack_and_send, 0)
-
+    for copy in inputs[1:]:
+        copy.wait()
     normal[...] = jnp.zeros_like(normal)
     for k in range(6):
         for axis in range(3):
             normal[axis, k : k + 1, :] = area_ref[3 * k + axis : 3 * k + axis + 1, :]
     areas = jnp.sqrt(normal[0] * normal[0] + normal[1] * normal[1] + normal[2] * normal[2])
-    volume = volume_ref[...]
+    volume = volume_ref[...].reshape(1, CELLS)
     limit = volume / (TOP_SPEED * jnp.sum(areas, axis=0, keepdims=True))
     least = jnp.minimum(
         jnp.minimum(limit[:, 0:128], limit[:, 128:256]),
         jnp.minimum(limit[:, 256:384], limit[:, 384:512]),
     )
     min_msg[...] = jnp.broadcast_to(least, (8, 128))
+
+    pl.semaphore_wait(barrier, len(greeted))
     for copy in near_copies:
         copy.start()
+    start_sends(0)
+
+    def pack_next(c, _):
+        load(c).wait()
+        pack(c)
+
+        @pl.when(c < WINDOW)
+        def _():
+            start_sends(c)
+
+        return 0
+
+    lax.fori_loop(1, CHUNKS, pack_next, 0)
 
     speed = lax.broadcasted_iota(jnp.int32, (NODES, CELLS), 0).astype(F32) - HALF
     for k in range(6):
@@ -205,7 +240,7 @@
 
     for i in range(14):
         start = min(i * 128, VELS - 128)
-        row = stream_ref[:, start : start + 128]
+        row = stream_ref[start : start + 128].reshape(1, 128)
         stream_b[start : start + 128, :] = jnp.broadcast_to(row, (128, 128)).T
 
     def fill(i, _):
@@ -217,6 +252,15 @@
         return 0
 
     lax.fori_loop(0, 48, fill, 0)
+
+    for copy in near_copies:
+        copy.wait()
+    lowest = min_msg[...]
+    for i in range(near - 1):
+        lowest = jnp.minimum(lowest, min_in[i])
+    min_msg2[...] = lowest
+    for copy in far_copies:
+        copy.start()
 
     sums[...] = jnp.zeros_like(sums)
 
@@ -255,15 +299,6 @@
         old_msg[i : i + 1, :] = jnp.sum(sums[i], axis=0, keepdims=True)
     for copy in x_copies:
         copy.start()
-    for copy in near_copies:
-        copy.wait()
-    lowest = min_msg[...]
-    for i in range(near - 1):
-        lowest = jnp.minimum(lowest, min_in[i])
-    min_msg2[...] = lowest
-    for copy in far_copies:
-        copy.start()
-
     def products(lhs, half):
         for k in range(6):
             gathered[k] = jnp.dot(
@@ -302,12 +337,8 @@
         lax.fori_loop(0, GROUPS, one_group, 0)
         return 0
 
-    lax.fori_loop(0, CHUNKS, local_flux, 0)
-
-    for copy in x_copies:
-        copy.wait()
-    old_msg2[...] = old_msg[...] + old_in[0] + old_in[1] + old_in[2]
-    z_copy.start()
+    lax.fori_loop(0, AHEAD, local_flux, 0)
+
     for copy in far_copies:
         copy.wait()
     lowest = min_msg2[...]
@@ -322,8 +353,27 @@
 
     def remote_flux(c, _):
         rows = pl.ds(pl.multiple_of(c * CHUNK, CHUNK), CHUNK)
+
+        @pl.when(c + AHEAD < CHUNKS)
+        def _():
+            local_flux(c + AHEAD, 0)
+
         for d in range(4):
             send(c, d).wait_recv()
+
+        @pl.when(c + WINDOW < CHUNKS)
+        def _():
+            for d in range(4):
+                send(c, d).wait_send()
+            start_sends(c + WINDOW)
+
+        @pl.when(c == 4)
+        def _():
+            for copy in x_copies:
+                copy.wait()
+            old_msg2[...] = old_msg[...] + old_in[0] + old_in[1] + old_in[2]
+            z_copy.start()
+
         for d in range(4):
             high, low = two_parts(arrived[d, rows, :])
             lanes = slice(d * SEND, (d + 1) * SEND)
@@ -383,7 +433,7 @@
             send(c, d).wait_send()
         return 0
 
-    lax.fori_loop(0, CHUNKS, finish_sends, 0)
+    lax.fori_loop(CHUNKS - WINDOW, CHUNKS, finish_sends, 0)
     for copy in new_copies:
         copy.wait()
     total = new_msg[...]
@@ -453,6 +503,7 @@
     n_space = mesh.shape["space"]
     vmem = pl.BlockSpec(memory_space=pltpu.VMEM)
     hbm = pl.BlockSpec(memory_space=pl.ANY)
+    raw = pl.BlockSpec(memory_space=pltpu.HBM)
 
     def local(dist, free_stream, area_normal, cell_volume, face_nbr, face_type, send_list):
         moved, coef = pl.pallas_call(
@@ -461,9 +512,15 @@
                 jax.ShapeDtypeStruct((VELS, CELLS), F32),
                 jax.ShapeDtypeStruct((16, CELLS), F32),
             ),
-            in_specs=[hbm] + [vmem] * 6,
+            in_specs=[raw] * 7,
             out_specs=(vmem, vmem),
             scratch_shapes=[
+                pltpu.VMEM((VELS,), F32),
+                pltpu.VMEM((18, CELLS), F32),
+                pltpu.VMEM((CELLS,), F32),
+                pltpu.VMEM((6, CELLS), jnp.int32),
+                pltpu.VMEM((6, CELLS), jnp.int32),
+                pltpu.VMEM((4, SEND), jnp.int32),
                 pltpu.VMEM((VELS, CELLS), F32),
                 pltpu.VMEM((CHUNKS, 2 * CHUNK, CELLS), BF16),
                 pltpu.VMEM((4, VELS, SEND), F32),
@@ -489,6 +546,7 @@
                 pltpu.VMEM((8, 128), F32),
                 pltpu.VMEM((max(1, n_space // 8 - 1), 8, 128), F32),
                 pltpu.SemaphoreType.DMA((CHUNKS,)),
+                pltpu.SemaphoreType.DMA((6,)),
                 pltpu.SemaphoreType.DMA((CHUNKS, 4)),
                 pltpu.SemaphoreType.DMA((CHUNKS, 4)),
                 pltpu.SemaphoreType.DMA((21,)),
@@ -499,13 +557,18 @@
             ),
             name="transport",
         )(
-            dist,
-            free_stream.reshape(1, VELS),
-            area_normal,
-            cell_volume.reshape(1, CELLS),
-            face_nbr,
-            face_type,
-            send_list,
+            *[
+                pltpu.with_memory_space_constraint(x, pltpu.HBM)
+                for x in (
+                    dist,
+                    free_stream,
+                    area_normal,
+                    cell_volume,
+                    face_nbr,
+                    face_type,
+                    send_list,
+                )
+            ]
         )
         return pl.pallas_call(
             relax,

time: 125 us -> 83 us (0.66)
  Pallas kernels: 119 us -> 82.9 us
  local copies, waits for them, and re-layouts: 6.3 us -> 0 us
    pallas_call x1, Pallas kernels: 115 us -> 79.6 us  [local(): pl.pallas_call(functools.partial(transport, n_space), out_shape=(jax.Shap...]
    unnamed x12 -> x0, local copies, waits for them, and re-layouts: 5.59 us -> none
where the time goes in v2:
time: 83 us; the launch traced here: 82.9 us
  Pallas kernels  82.9 us (100%)
    pallas_call x1, Pallas kernels, local(): pl.pallas_call(functools.partial(transport, n_space), out_shape=(jax.Shap...  79.6 us
    pallas_call x1, Pallas kernels, local(): pl.pallas_call(relax, out_shape=jax.ShapeDtypeStruct((VELS, CELLS), F32),...  3.32 us

profile of v2, /device:TPU:1, one launch (start us, length us, event | category | flops | bytes accessed | tf_op | source)
XLA Modules:
  0.0 82.9 jit_solution(17649114117301122501)
XLA Ops:
  0.0 79.6 %transport.1 = (f32[1728,512]{1,0:T(8,128)S(1)}, f32[16,512]{1,0:T(8,128)S(1)}) custom-call(f32[1728,512]{1,0:T(8,128)} %dist_hbm.1, f32[1728]{0:T(1024)} %stream_hbm.1, f32[18,512]{1,0:T(8,128)} %area_hbm.1, f32[512]{0:T(512)} %volume_hbm.1, s32[6,512]{1,0:T(8,128)} %nbr_hbm.1, s32[6,512]{1,0:T(8,128)} %type_hbm.1, s32[4,128]{1,0:T(4,128)} %list_hbm.1), custom_call_target="tpu_custom_call" | custom-call | tf_op jit(solution)/shard_map/transport/pallas_call | solution.py:509
  79.6 3.3 %relax.1 = f32[1728,512]{1,0:T(8,128)} custom-call(f32[1728,512]{1,0:T(8,128)S(1)} %get-tuple-element.7.moved, f32[16,512]{1,0:T(8,128)S(1)} %get-tuple-element.8.coef_ref), custom_call_target="tpu_custom_call" | custom-call | tf_op jit(solution)/shard_map/relax/pallas_call | solution.py:573

commit v3 on v2

--- a/solution.py
+++ b/solution.py
@@ -27,8 +27,9 @@
 CHUNK = 144
 CHUNKS = VELS // CHUNK
 GROUPS = CHUNK // NODES
-WINDOW = 3
-AHEAD = 2
+FIRST = 3
+WINDOW = 12
+SPLIT = 6
 
 
 def two_parts(x):
@@ -61,6 +62,7 @@
     nbr_hbm,
     type_hbm,
     list_hbm,
+    dist_v,
     moved,
     coef_ref,
     stream_ref,
@@ -69,7 +71,6 @@
     nbr_ref,
     type_ref,
     list_ref,
-    dist_v,
     parts,
     outgoing,
     arrived,
@@ -190,11 +191,13 @@
             outgoing[d, rows, :] = picked[:, d * SEND : (d + 1) * SEND]
 
     def start_sends(c):
-        for d in range(4):
+        for d in (2, 3, 0, 1):
             send(c, d).start()
 
     load(0).wait()
     pack(0)
+    pl.semaphore_wait(barrier, len(greeted))
+    start_sends(0)
     for copy in inputs[1:]:
         copy.wait()
     normal[...] = jnp.zeros_like(normal)
@@ -204,28 +207,28 @@
     areas = jnp.sqrt(normal[0] * normal[0] + normal[1] * normal[1] + normal[2] * normal[2])
     volume = volume_ref[...].reshape(1, CELLS)
     limit = volume / (TOP_SPEED * jnp.sum(areas, axis=0, keepdims=True))
-    least = jnp.minimum(
+    lowest = jnp.minimum(
         jnp.minimum(limit[:, 0:128], limit[:, 128:256]),
         jnp.minimum(limit[:, 256:384], limit[:, 384:512]),
     )
-    min_msg[...] = jnp.broadcast_to(least, (8, 128))
-
-    pl.semaphore_wait(barrier, len(greeted))
+    min_msg[...] = lowest
     for copy in near_copies:
         copy.start()
-    start_sends(0)
-
-    def pack_next(c, _):
+
+    def pack_and_send(c, _):
         load(c).wait()
         pack(c)
-
-        @pl.when(c < WINDOW)
-        def _():
-            start_sends(c)
-
-        return 0
-
-    lax.fori_loop(1, CHUNKS, pack_next, 0)
+        start_sends(c)
+        return 0
+
+    lax.fori_loop(1, FIRST, pack_and_send, 0)
+
+    def pack_rest(c, _):
+        load(c).wait()
+        pack(c)
+        return 0
+
+    lax.fori_loop(FIRST, CHUNKS, pack_rest, 0)
 
     speed = lax.broadcasted_iota(jnp.int32, (NODES, CELLS), 0).astype(F32) - HALF
     for k in range(6):
@@ -252,15 +255,6 @@
         return 0
 
     lax.fori_loop(0, 48, fill, 0)
-
-    for copy in near_copies:
-        copy.wait()
-    lowest = min_msg[...]
-    for i in range(near - 1):
-        lowest = jnp.minimum(lowest, min_in[i])
-    min_msg2[...] = lowest
-    for copy in far_copies:
-        copy.start()
 
     sums[...] = jnp.zeros_like(sums)
 
@@ -297,12 +291,26 @@
     old_msg[...] = jnp.zeros_like(old_msg)
     for i in range(13):
         old_msg[i : i + 1, :] = jnp.sum(sums[i], axis=0, keepdims=True)
+    for copy in near_copies:
+        copy.wait()
+    lowest = min_msg[...]
+    for i in range(near - 1):
+        lowest = jnp.minimum(lowest, min_in[i])
+    min_msg2[...] = lowest
+    for copy in far_copies:
+        copy.start()
     for copy in x_copies:
         copy.start()
-    def products(lhs, half):
+
+    def send_next(c, _):
+        start_sends(c)
+        return 0
+
+    lax.fori_loop(FIRST, WINDOW, send_next, 0)
+    def products(lhs, first, last):
         for k in range(6):
             gathered[k] = jnp.dot(
-                lhs, picks[k, half * CELLS : (half + 1) * CELLS, :], preferred_element_type=F32
+                lhs, picks[k, first:last, :], preferred_element_type=F32
             )
 
     def picked_rows(k, g):
@@ -313,8 +321,20 @@
     def normal_speed(k, cx, cy):
         return (cx * normal[0, k : k + 1, :] + cy * normal[1, k : k + 1, :]) + slope[k]
 
-    def local_flux(c, _):
-        products(parts[c], 0)
+    def flux(c, local, remote):
+        if remote:
+            arrived_rows = pl.ds(pl.multiple_of(c * CHUNK, CHUNK), CHUNK)
+            for d in range(4):
+                high, low = two_parts(arrived[d, arrived_rows, :])
+                lanes = slice(d * SEND, (d + 1) * SEND)
+                arrived_parts[0:CHUNK, lanes] = high
+                arrived_parts[CHUNK : 2 * CHUNK, lanes] = low
+        if local and remote:
+            products(jnp.concatenate([parts[c], arrived_parts[...]], axis=1), 0, 2 * CELLS)
+        elif local:
+            products(parts[c], 0, CELLS)
+        else:
+            products(arrived_parts[...], CELLS, 2 * CELLS)
 
         def one_group(g, _):
             group = c * GROUPS + g
@@ -325,39 +345,39 @@
             total = jnp.zeros((NODES, CELLS), F32)
             for k in range(6):
                 u = jnp.minimum(normal_speed(k, cx, cy), 0.0)
-                inward += u
-                free += u * inflow[k : k + 1, :]
                 total += u * picked_rows(k, g)
-            stream = stream_b[rows, :]
-            stream = jnp.concatenate([stream] * 4, axis=1)
-            outward = normal_speed(6, cx, cy) - inward
-            moved[rows, :] = outward * dist_v[rows, :] + total + free * stream
+                if local:
+                    inward += u
+                    free += u * inflow[k : k + 1, :]
+            if local:
+                stream = stream_b[rows, :]
+                stream = jnp.concatenate([stream] * 4, axis=1)
+                outward = normal_speed(6, cx, cy) - inward
+                total += outward * dist_v[rows, :] + free * stream
+            else:
+                total += moved[rows, :]
+            moved[rows, :] = total
+            if remote:
+                t1 = total * speed
+                s0, s1, s2 = fold(total), fold(t1), fold(t1 * speed)
+                sums[0] += s0
+                sums[1] += cx * s0
+                sums[2] += cy * s0
+                sums[3] += s1
+                sums[4] += 0.5 * ((cx * cx + cy * cy) * s0 + s2)
             return 0
 
         lax.fori_loop(0, GROUPS, one_group, 0)
-        return 0
-
-    lax.fori_loop(0, AHEAD, local_flux, 0)
-
-    for copy in far_copies:
-        copy.wait()
-    lowest = min_msg2[...]
-    for i in range(far - 1):
-        lowest = jnp.minimum(lowest, min_in2[i])
-    time_step = CFL * jnp.min(lowest[0:1, :], axis=1, keepdims=True)
-    time_step = jnp.broadcast_to(time_step, (1, CELLS))
-    ratio = time_step / volume
-
+
+    def local_part(c, _):
+        flux(c, True, False)
+        return 0
+
+    lax.fori_loop(SPLIT, CHUNKS, local_part, 0)
     for i in range(5):
         sums[i] = jnp.zeros((8, CELLS), F32)
 
-    def remote_flux(c, _):
-        rows = pl.ds(pl.multiple_of(c * CHUNK, CHUNK), CHUNK)
-
-        @pl.when(c + AHEAD < CHUNKS)
-        def _():
-            local_flux(c + AHEAD, 0)
-
+    def arrive(c):
         for d in range(4):
             send(c, d).wait_recv()
 
@@ -366,6 +386,9 @@
             for d in range(4):
                 send(c, d).wait_send()
             start_sends(c + WINDOW)
+
+    def whole_part(c, _):
+        arrive(c)
 
         @pl.when(c == 4)
         def _():
@@ -374,43 +397,33 @@
             old_msg2[...] = old_msg[...] + old_in[0] + old_in[1] + old_in[2]
             z_copy.start()
 
-        for d in range(4):
-            high, low = two_parts(arrived[d, rows, :])
-            lanes = slice(d * SEND, (d + 1) * SEND)
-            arrived_parts[0:CHUNK, lanes] = high
-            arrived_parts[CHUNK : 2 * CHUNK, lanes] = low
-        products(arrived_parts[...], 1)
-
-        def one_group(g, _):
-            group = c * GROUPS + g
-            own = pl.ds(pl.multiple_of(group * NODES, NODES), NODES)
-            cx, cy = group_speeds(v, group)
-            total = moved[own, :]
-            for k in range(6):
-                u = jnp.minimum(normal_speed(k, cx, cy), 0.0)
-                total += u * picked_rows(k, g)
-            t = dist_v[own, :] - ratio * total
-            moved[own, :] = t
-            t1 = t * speed
-            s0, s1, s2 = fold(t), fold(t1), fold(t1 * speed)
-            sums[0] += s0
-            sums[1] += cx * s0
-            sums[2] += cy * s0
-            sums[3] += s1
-            sums[4] += 0.5 * ((cx * cx + cy * cy) * s0 + s2)
-            return 0
-
-        lax.fori_loop(0, GROUPS, one_group, 0)
-        return 0
-
-    lax.fori_loop(0, CHUNKS, remote_flux, 0)
+        flux(c, True, True)
+        return 0
+
+    lax.fori_loop(0, SPLIT, whole_part, 0)
+
+    def remote_part(c, _):
+        arrive(c)
+        flux(c, False, True)
+        return 0
+
+    lax.fori_loop(SPLIT, CHUNKS, remote_part, 0)
 
     new_msg[...] = jnp.zeros_like(new_msg)
     for i in range(5):
-        new_msg[i : i + 1, :] = jnp.sum(sums[i], axis=0, keepdims=True)
+        row = jnp.sum(sums[i], axis=0, keepdims=True)
+        for t in range(4):
+            new_msg[4 * i + t : 4 * i + t + 1, :] = row[:, 128 * t : 128 * t + 128]
     for copy in new_copies:
         copy.start()
 
+    for copy in far_copies:
+        copy.wait()
+    lowest = min_msg2[...]
+    for i in range(far - 1):
+        lowest = jnp.minimum(lowest, min_in2[i])
+    time_step = CFL * jnp.min(lowest, axis=1, keepdims=True)
+    time_step = jnp.broadcast_to(time_step, (1, CELLS))
     z_copy.wait()
     old = old_msg2[...] + old_in2[...]
     rho = old[0:1]
@@ -425,8 +438,11 @@
         coef_ref[8 + i : 9 + i, :] = 0.5 * (
             old[10 + i : 11 + i] - 2.0 * along - mean[i] * trace + 2.0 * rho * mean_sq * mean[i]
         )
-    coef_ref[11:12, :] = time_step
-    coef_ref[12:16, :] = jnp.zeros((4, CELLS), F32)
+    ratio = time_step / volume
+    coef_ref[5:6, :] = ratio
+    coef_ref[6:7, :] = time_step
+    coef_ref[7:8, :] = jnp.zeros((1, CELLS), F32)
+    coef_ref[11:16, :] = jnp.zeros((5, CELLS), F32)
 
     def finish_sends(c, _):
         for d in range(4):
@@ -439,15 +455,20 @@
     total = new_msg[...]
     for i in range(7):
         total = total + new_in[i]
-    coef_ref[0:8, :] = total
-
-
-def relax(moved, coef_ref, out_hbm, result, first, second, third, sem):
+    energy = 0.5 * trace
+    for i in range(5):
+        phi = jnp.concatenate([total[4 * i + t : 4 * i + t + 1] for t in range(4)], axis=1)
+        before = energy if i == 4 else old[i : i + 1]
+        coef_ref[i : i + 1, :] = before - ratio * phi
+
+
+def relax(dist_v, moved, coef_ref, out_hbm, result, first, second, third, sem):
     v = lax.axis_index("vel")
     rho = coef_ref[0:1, :]
     mean = [coef_ref[1 + i : 2 + i, :] / rho for i in range(3)]
     heat = [coef_ref[8 + i : 9 + i, :] for i in range(3)]
-    time_step = coef_ref[11:12, :]
+    ratio = coef_ref[5:6, :]
+    time_step = coef_ref[6:7, :]
     mean_sq = mean[0] * mean[0] + mean[1] * mean[1] + mean[2] * mean[2]
     temp = (2.0 * coef_ref[4:5, :] / rho - mean_sq) / 3.0
     relax_time = MU_REF * jnp.exp(OMEGA * jnp.log(temp)) / (rho * temp)
@@ -481,7 +502,8 @@
             sq = (first[1, a, :] + second[1, b, :]) + third[1]
             along = (first[2, a, :] + second[2, b, :]) + third[2]
             gauss = weight * third[0]
-            result[rows, :] = moved[rows, :] * keep + gauss * (1.0 + along * sq)
+            rest = dist_v[rows, :] - ratio * moved[rows, :]
+            result[rows, :] = rest * keep + gauss * (1.0 + along * sq)
             return 0
 
         lax.fori_loop(0, GROUPS, one_group, 0)
@@ -506,14 +528,15 @@
     raw = pl.BlockSpec(memory_space=pltpu.HBM)
 
     def local(dist, free_stream, area_normal, cell_volume, face_nbr, face_type, send_list):
-        moved, coef = pl.pallas_call(
+        own, moved, coef = pl.pallas_call(
             functools.partial(transport, n_space),
             out_shape=(
+                jax.ShapeDtypeStruct((VELS, CELLS), F32),
                 jax.ShapeDtypeStruct((VELS, CELLS), F32),
                 jax.ShapeDtypeStruct((16, CELLS), F32),
             ),
             in_specs=[raw] * 7,
-            out_specs=(vmem, vmem),
+            out_specs=(vmem, vmem, vmem),
             scratch_shapes=[
                 pltpu.VMEM((VELS,), F32),
                 pltpu.VMEM((18, CELLS), F32),
@@ -521,7 +544,6 @@
                 pltpu.VMEM((6, CELLS), jnp.int32),
                 pltpu.VMEM((6, CELLS), jnp.int32),
                 pltpu.VMEM((4, SEND), jnp.int32),
-                pltpu.VMEM((VELS, CELLS), F32),
                 pltpu.VMEM((CHUNKS, 2 * CHUNK, CELLS), BF16),
                 pltpu.VMEM((4, VELS, SEND), F32),
                 pltpu.VMEM((4, VELS, SEND), F32),
@@ -539,12 +561,12 @@
                 pltpu.VMEM((3, 16, CELLS), F32),
                 pltpu.VMEM((16, CELLS), F32),
                 pltpu.VMEM((16, CELLS), F32),
-                pltpu.VMEM((8, CELLS), F32),
-                pltpu.VMEM((7, 8, CELLS), F32),
-                pltpu.VMEM((8, 128), F32),
-                pltpu.VMEM((7, 8, 128), F32),
-                pltpu.VMEM((8, 128), F32),
-                pltpu.VMEM((max(1, n_space // 8 - 1), 8, 128), F32),
+                pltpu.VMEM((24, 128), F32),
+                pltpu.VMEM((7, 24, 128), F32),
+                pltpu.VMEM((1, 128), F32),
+                pltpu.VMEM((7, 1, 128), F32),
+                pltpu.VMEM((1, 128), F32),
+                pltpu.VMEM((n_space // 8 - 1, 1, 128), F32),
                 pltpu.SemaphoreType.DMA((CHUNKS,)),
                 pltpu.SemaphoreType.DMA((6,)),
                 pltpu.SemaphoreType.DMA((CHUNKS, 4)),
@@ -573,7 +595,7 @@
         return pl.pallas_call(
             relax,
             out_shape=jax.ShapeDtypeStruct((VELS, CELLS), F32),
-            in_specs=[vmem, vmem],
+            in_specs=[vmem] * 3,
             out_specs=hbm,
             scratch_shapes=[
                 pltpu.VMEM((VELS, CELLS), F32),
@@ -584,7 +606,7 @@
             ],
             compiler_params=pltpu.CompilerParams(vmem_limit_bytes=24 * 2**20),
             name="relax",
-        )(moved, coef)
+        )(own, moved, coef)
 
     return jax.shard_map(
         local,

time: 83 us -> 81.1 us (0.977)
  Pallas kernels: 82.9 us -> 80.4 us
    pallas_call x1, Pallas kernels: 79.6 us -> 77 us  [local(): pl.pallas_call(functools.partial(transport, n_space), out_shape=(jax.Shap...]
where the time goes in v3:
time: 81.1 us; the launch traced here: 80.4 us
  Pallas kernels  80.4 us (99%)
    pallas_call x1, Pallas kernels, local(): pl.pallas_call(functools.partial(transport, n_space), out_shape=(jax.Shap...  77 us
    pallas_call x1, Pallas kernels, local(): pl.pallas_call(relax, out_shape=jax.ShapeDtypeStruct((VELS, CELLS), F32),...  3.32 us

profile of v3, /device:TPU:1, one launch (start us, length us, event | category | flops | bytes accessed | tf_op | source)
XLA Modules:
  0.0 80.4 jit_solution(5460505770347687689)
XLA Ops:
  0.0 77.0 %transport.1 = (f32[1728,512]{1,0:T(8,128)S(1)}, f32[1728,512]{1,0:T(8,128)S(1)}, f32[16,512]{1,0:T(8,128)S(1)}) custom-call(f32[1728,512]{1,0:T(8,128)} %dist_hbm.1, f32[1728]{0:T(1024)} %stream_hbm.1, f32[18,512]{1,0:T(8,128)} %area_hbm.1, f32[512]{0:T(512)} %volume_hbm.1, s32[6,512]{1,0:T(8,128)} %nbr_hbm.1, s32[6,512]{1,0:T(8,128)} %type_hbm.1, ...), custom_call_target="tpu_custom_call" | custom-call | tf_op jit(solution)/shard_map/transport/pallas_call | solution.py:531
  77.0 3.3 %relax.1 = f32[1728,512]{1,0:T(8,128)} custom-call(f32[1728,512]{1,0:T(8,128)S(1)} %get-tuple-element.8.dist_v, f32[1728,512]{1,0:T(8,128)S(1)} %get-tuple-element.9.moved, f32[16,512]{1,0:T(8,128)S(1)} %get-tuple-element.10.coef_ref), custom_call_target="tpu_custom_call" | custom-call | tf_op jit(solution)/shard_map/relax/pallas_call | solution.py:595

commit v4 on v3

--- a/solution.py
+++ b/solution.py
@@ -28,7 +28,6 @@
 CHUNKS = VELS // CHUNK
 GROUPS = CHUNK // NODES
 FIRST = 3
-WINDOW = 12
 SPLIT = 6
 
 
@@ -108,7 +107,7 @@
     partners = [lax.rem(s + step + n_space, n_space) for step in STEPS]
     near_peers = [(s // near) * near + lax.rem(s + i, near) for i in range(1, near)]
     far_peers = [lax.rem(s + near * i, n_space) for i in range(1, far)]
-    vel_peers = [lax.rem(v + i, 8) for i in range(1, 8)]
+    vel_peers = [lax.rem(v + i, 8) for i in (4, 5, 3, 6, 2, 7, 1)]
     x_peers = [lax.rem(v + 2 * i, 8) for i in range(1, 4)]
     z_peer = v + 1 - 2 * lax.rem(v, 2)
 
@@ -306,7 +305,7 @@
         start_sends(c)
         return 0
 
-    lax.fori_loop(FIRST, WINDOW, send_next, 0)
+    lax.fori_loop(FIRST, CHUNKS, send_next, 0)
     def products(lhs, first, last):
         for k in range(6):
             gathered[k] = jnp.dot(
@@ -367,7 +366,7 @@
                 sums[4] += 0.5 * ((cx * cx + cy * cy) * s0 + s2)
             return 0
 
-        lax.fori_loop(0, GROUPS, one_group, 0)
+        lax.fori_loop(0, GROUPS, one_group, 0, unroll=2)
 
     def local_part(c, _):
         flux(c, True, False)
@@ -380,12 +379,6 @@
     def arrive(c):
         for d in range(4):
             send(c, d).wait_recv()
-
-        @pl.when(c + WINDOW < CHUNKS)
-        def _():
-            for d in range(4):
-                send(c, d).wait_send()
-            start_sends(c + WINDOW)
 
     def whole_part(c, _):
         arrive(c)
@@ -402,9 +395,15 @@
 
     lax.fori_loop(0, SPLIT, whole_part, 0)
 
+    def finish_sends(c, _):
+        for d in range(4):
+            send(c, d).wait_send()
+        return 0
+
     def remote_part(c, _):
         arrive(c)
         flux(c, False, True)
+        finish_sends(c - SPLIT, 0)
         return 0
 
     lax.fori_loop(SPLIT, CHUNKS, remote_part, 0)
@@ -444,17 +443,13 @@
     coef_ref[7:8, :] = jnp.zeros((1, CELLS), F32)
     coef_ref[11:16, :] = jnp.zeros((5, CELLS), F32)
 
-    def finish_sends(c, _):
-        for d in range(4):
-            send(c, d).wait_send()
-        return 0
-
-    lax.fori_loop(CHUNKS - WINDOW, CHUNKS, finish_sends, 0)
-    for copy in new_copies:
-        copy.wait()
+    lax.fori_loop(CHUNKS - SPLIT, CHUNKS, finish_sends, 0)
     total = new_msg[...]
     for i in range(7):
+        new_copies[i].wait_recv()
         total = total + new_in[i]
+    for copy in new_copies:
+        copy.wait_send()
     energy = 0.5 * trace
     for i in range(5):
         phi = jnp.concatenate([total[4 * i + t : 4 * i + t + 1] for t in range(4)], axis=1)
@@ -506,7 +501,7 @@
             result[rows, :] = rest * keep + gauss * (1.0 + along * sq)
             return 0
 
-        lax.fori_loop(0, GROUPS, one_group, 0)
+        lax.fori_loop(0, GROUPS, one_group, 0, unroll=True)
         rows = pl.ds(pl.multiple_of(c * CHUNK, CHUNK), CHUNK)
         pltpu.make_async_copy(result.at[rows], out_hbm.at[rows], sem.at[c]).start()
         return 0

time: 81.1 us -> 79.5 us (0.980)
  Pallas kernels: 80.4 us -> 79.1 us
where the time goes in v4:
time: 79.5 us; the launch traced here: 79.1 us
  Pallas kernels  79.1 us (99%)
    pallas_call x1, Pallas kernels, local(): pl.pallas_call(functools.partial(transport, n_space), out_shape=(jax.Shap...  76.3 us
    pallas_call x1, Pallas kernels, local(): pl.pallas_call(relax, out_shape=jax.ShapeDtypeStruct((VELS, CELLS), F32),...  2.81 us

profile of v4, /device:TPU:1, one launch (start us, length us, event | category | flops | bytes accessed | tf_op | source)
XLA Modules:
  0.0 79.1 jit_solution(14190266903564043718)
XLA Ops:
  0.0 76.3 %transport.1 = (f32[1728,512]{1,0:T(8,128)S(1)}, f32[1728,512]{1,0:T(8,128)S(1)}, f32[16,512]{1,0:T(8,128)S(1)}) custom-call(f32[1728,512]{1,0:T(8,128)} %dist_hbm.1, f32[1728]{0:T(1024)} %stream_hbm.1, f32[18,512]{1,0:T(8,128)} %area_hbm.1, f32[512]{0:T(512)} %volume_hbm.1, s32[6,512]{1,0:T(8,128)} %nbr_hbm.1, s32[6,512]{1,0:T(8,128)} %type_hbm.1, ...), custom_call_target="tpu_custom_call" | custom-call | tf_op jit(solution)/shard_map/transport/pallas_call | solution.py:526
  76.3 2.8 %relax.1 = f32[1728,512]{1,0:T(8,128)} custom-call(f32[1728,512]{1,0:T(8,128)S(1)} %get-tuple-element.8.dist_v, f32[1728,512]{1,0:T(8,128)S(1)} %get-tuple-element.9.moved, f32[16,512]{1,0:T(8,128)S(1)} %get-tuple-element.10.coef_ref), custom_call_target="tpu_custom_call" | custom-call | tf_op jit(solution)/shard_map/relax/pallas_call | solution.py:590

commit v5 on v4

--- a/solution.py
+++ b/solution.py
@@ -366,7 +366,7 @@
                 sums[4] += 0.5 * ((cx * cx + cy * cy) * s0 + s2)
             return 0
 
-        lax.fori_loop(0, GROUPS, one_group, 0, unroll=2)
+        lax.fori_loop(0, GROUPS, one_group, 0, unroll=3)
 
     def local_part(c, _):
         flux(c, True, False)

time: 79.5 us -> 79.4 us (level)
  no operation moved by 1% of the time
where the time goes in v5:
time: 79.4 us; the launch traced here: 79.1 us
  Pallas kernels  79.1 us (100%)
    pallas_call x1, Pallas kernels, local(): pl.pallas_call(functools.partial(transport, n_space), out_shape=(jax.Shap...  76.3 us
    pallas_call x1, Pallas kernels, local(): pl.pallas_call(relax, out_shape=jax.ShapeDtypeStruct((VELS, CELLS), F32),...  2.81 us

profile of v5, /device:TPU:1, one launch (start us, length us, event | category | flops | bytes accessed | tf_op | source)
XLA Modules:
  0.0 79.1 jit_solution(1492106090437294008)
XLA Ops:
  0.0 76.3 %transport.1 = (f32[1728,512]{1,0:T(8,128)S(1)}, f32[1728,512]{1,0:T(8,128)S(1)}, f32[16,512]{1,0:T(8,128)S(1)}) custom-call(f32[1728,512]{1,0:T(8,128)} %dist_hbm.1, f32[1728]{0:T(1024)} %stream_hbm.1, f32[18,512]{1,0:T(8,128)} %area_hbm.1, f32[512]{0:T(512)} %volume_hbm.1, s32[6,512]{1,0:T(8,128)} %nbr_hbm.1, s32[6,512]{1,0:T(8,128)} %type_hbm.1, ...), custom_call_target="tpu_custom_call" | custom-call | tf_op jit(solution)/shard_map/transport/pallas_call | solution.py:526
  76.3 2.8 %relax.1 = f32[1728,512]{1,0:T(8,128)} custom-call(f32[1728,512]{1,0:T(8,128)S(1)} %get-tuple-element.8.dist_v, f32[1728,512]{1,0:T(8,128)S(1)} %get-tuple-element.9.moved, f32[16,512]{1,0:T(8,128)S(1)} %get-tuple-element.10.coef_ref), custom_call_target="tpu_custom_call" | custom-call | tf_op jit(solution)/shard_map/relax/pallas_call | solution.py:590
